TPU v7x, 512 devices: a whole 4x4x16 slice. The times are simulated.
512 devices in a mesh: section: 8 (over z_hi, core), expert: 64 (over x, y, z_lo).
Axes of the slice: x: 4, y: 4, z: 16 (z_hi: 4, z_lo: 4; z = z_hi * 4 + z_lo), core: 2. Of those that a mesh axis runs over, the one named last changes fastest.
Arguments:
- hidden_rows: bfloat16 [8, 4096, 3584], P('section', 'expert'), may hold values from -6 to 6
- norm_gain: float32 [8, 3584], P('section'), may hold values from 0.1 to 1.9
- routes: int32 [8, 4096, 2], P('section', 'expert'), may hold values from 0 to 7, all different within a row; in each aligned block of 64 rows (0 to 63, 64 to 127, ..., all dimensions but the last counted through in order) at most 16 rows name the same one
- gates: float32 [8, 4096, 2], P('section', 'expert'), may hold values from 0.1 to 0.6
- w_gate_up: bfloat16 [8, 64, 3584, 256], P('section', 'expert'), may hold values from -0.09375 to 0.09375
- w_down: bfloat16 [8, 64, 128, 3584], P('section', 'expert'), may hold values from -0.1875 to 0.1875
Outputs:
- handoff: bfloat16 [8, 4096, 3584], P('section', 'expert')
Inputs may be any that keep to these rules, and one draw needn't show every extreme that they name: `routes`: in the rows of one device, every expert is named exactly 16 times.
All inputs are finite; a program needn't handle non-finite values.
Results may differ from a plain program's by a relative error of at most 0.004.
Values may be sent and summed in bfloat16 or wider, within the bound.
A program may use at most 64 MiB of HBM per device.

v0:
```python
import jax
import jax.numpy as jnp
from jax import lax
from jax.sharding import PartitionSpec as P

EXPERTS = 8


def passed_along(x, axis, by):
    size = lax.axis_size(axis)
    return lax.ppermute(x, axis, [(i, (i + by) % size) for i in range(size)])


def routed_part(hidden_rows, norm_gain, routes, gates, w_gate_up, w_down):
    rows_in = hidden_rows[0]
    tok_rows = rows_in.shape[0]
    width = rows_in.shape[1]
    picks = routes.shape[2]
    owners = lax.axis_size("expert")
    shard_count = owners // EXPERTS
    capacity = tok_rows * picks // EXPERTS
    inner = w_down.shape[2]
    rows_f32 = rows_in.astype(jnp.float32)
    normed = (
        rows_f32
        * lax.rsqrt(jnp.mean(rows_f32 * rows_f32, axis=1, keepdims=True) + 1e-06)
        * norm_gain[0][None, :]
    ).astype(jnp.bfloat16)
    expert_ids = routes[0].reshape(-1)
    one_hot = (expert_ids[:, None] == jnp.arange(EXPERTS, dtype=jnp.int32)[None, :]).astype(
        jnp.int32
    )
    earlier = jnp.cumsum(one_hot, axis=0) - one_hot
    slot_id = jnp.sum(earlier * one_hot, axis=1)
    target = expert_ids * capacity + slot_id
    placing = (jnp.arange(EXPERTS * capacity, dtype=jnp.int32)[:, None] == target[None, :]).astype(
        jnp.bfloat16
    )
    repeated = jnp.repeat(normed, picks, axis=0)
    by_expert = (
        jnp.dot(placing, repeated, preferred_element_type=jnp.float32)
        .astype(jnp.bfloat16)
        .reshape(EXPERTS, capacity, width)
    )
    outgoing = jnp.repeat(by_expert, shard_count, axis=0)
    received = lax.all_to_all(outgoing, "expert", split_axis=0, concat_axis=0, tiled=True)
    slots = received.shape[1]
    flat_rows = received.reshape(-1, width)
    gate_up = jnp.dot(flat_rows, w_gate_up[0, 0], preferred_element_type=jnp.float32)
    activated = (jax.nn.silu(gate_up[:, :inner]) * gate_up[:, inner:]).astype(jnp.bfloat16)
    partial_value = jnp.dot(activated, w_down[0, 0], preferred_element_type=jnp.float32).astype(
        jnp.bfloat16
    )
    returned = lax.all_to_all(
        partial_value.reshape(owners, slots, width),
        "expert",
        split_axis=0,
        concat_axis=0,
        tiled=True,
    )
    expert_sum = jnp.sum(
        returned.reshape(EXPERTS, shard_count, capacity, width), axis=1, dtype=jnp.float32
    )
    collected = expert_sum.reshape(EXPERTS * capacity, width)[target]
    routed_sum = jnp.sum(collected.reshape(tok_rows, picks, width) * gates[0][:, :, None], axis=1)
    return (rows_f32, routed_sum)


def local(hidden_rows, norm_gain, routes, gates, w_gate_up, w_down):
    rows_f32, routed_sum = routed_part(hidden_rows, norm_gain, routes, gates, w_gate_up, w_down)
    layer_out = (rows_f32 + routed_sum).astype(jnp.bfloat16)[None]
    handoff = passed_along(layer_out, "section", 1)
    return handoff


def solution(mesh):
    in_specs = (
        P("section", "expert", None),
        P("section", None),
        P("section", "expert", None),
        P("section", "expert", None),
        P("section", "expert", None, None),
        P("section", "expert", None, None),
    )
    out_specs = P("section", "expert", None)
    return jax.shard_map(local, mesh=mesh, in_specs=in_specs, out_specs=out_specs, check_vma=False)
```

profile of v0, /device:TPU:1, one launch (start us, length us, event | category | flops | bytes accessed | tf_op | source)
XLA Modules:
  0.0 406.4 jit_solution(5856779225343671979)
XLA Ops:
  0.0 0.0 copy-start
  0.0 0.9 copy.10
  0.9 0.1 reshape_squeeze.3
  1.0 0.1 fusion.12
  1.1 0.2 reduce_window_sum.11
  1.3 0.2 select_reduce_fusion
  1.5 1.2 fusion.4
  2.7 0.8 reduce
  3.5 1.2 fusion.6
  4.7 1.4 broadcast_in_dim.4
  6.1 2.5 reshape.73
  8.6 0.4 convolution_convert_fusion.1
  9.0 0.9 broadcast_in_dim.5
  9.9 175.4 %all_to_all.10 = bf16[64,16,3584]{2,1,0:T(8,128)(2,1)S(1)} all-to-all(bf16[64,16,3584]{2,1,0:T(8,128)(2,1)S(1)} %bitcast.39), channel_id=1, replica_groups=mesh['section'=8,'expert'=64] {'expert'}, dimensions={0} | all-to-all | bytes 14680064 | tf_op jit(solution)/shard_map/all_to_all | solution.py:46
  185.3 0.0 copy-done
  185.3 2.1 fusion
  187.3 5.1 %convolution_convert_fusion = bf16[1024,3584]{1,0:T(8,128)(2,1)} fusion(bf16[1,1,128,3584]{3,2,1,0:T(8,128)(2,1)S(1)} %copy-done.2, f32[1024,256]{1,0:T(8,128)S(1)} %fusion), kind=kOutput, calls=%fused_computation.2 | convolution fusion | flops 943980544 | bytes 9306112 | tf_op jit(solution)/shard_map/dot_general | solution.py:51
  192.4 6.0 %all-to-all-start.1 = ((bf16[64,16,3584]{2,1,0:T(8,128)(2,1)}), bf16[64,16,3584]{2,1,0:T(8,128)(2,1)}, u32[]{:S(2)}, u32[]{:S(2)}) async-start(bf16[64,16,3584]{2,1,0:T(8,128)(2,1)} %bitcast.38), calls=%async_computation.1 | async-start | bytes 14680064 | tf_op jit(solution)/shard_map/all_to_all | solution.py:54
  198.5 0.1 copy.11
  198.6 0.1 mul.78
  198.7 0.0 copy-done.4
  198.7 0.1 copy.12
  198.8 161.2 %all-to-all-done.1 = bf16[64,16,3584]{2,1,0:T(8,128)(2,1)} async-done(((bf16[64,16,3584]{2,1,0:T(8,128)(2,1)}), bf16[64,16,3584]{2,1,0:T(8,128)(2,1)}, u32[]{:S(2)}, u32[]{:S(2)}) %all-to-all-start.1) | async-done | bytes 7340064 | tf_op jit(solution)/shard_map/all_to_all | solution.py:54
  360.0 5.8 %convert_reduce_fusion = f32[8,16,3584]{2,1,0:T(8,128)} fusion(bf16[64,16,3584]{2,1,0:T(8,128)(2,1)} %all-to-all-done.1), kind=kLoop, calls=%fused_computation.1 | loop fusion | flops 6881280 | bytes 9175040 | tf_op jit(solution)/shard_map/reduce_sum | solution.py:61
  365.8 4.7 %gather_fusion = f32[128,3584]{1,0:T(8,128)} fusion(f32[128,3584]{1,0:T(8,128)} %bitcast.37, s32[1024]{0:T(1024)S(1)} %pad_clamp_fusion), kind=kCustom, calls=%fused_computation | custom fusion | bytes 3670528 | tf_op jit(solution)/shard_map/gather | solution.py:64
  370.5 3.3 reshape.79
  373.7 4.1 %multiply_reduce_fusion = f32[64,3584]{1,0:T(8,128)S(1)} fusion(f32[64,2,3584]{2,1,0:T(2,128)} %reshape.79, f32[64,2]{1,0:T(8,128)S(1)} %copy.12), kind=kLoop, calls=%fused_computation.6 | loop fusion | flops 688128 | bytes 2753024 | tf_op jit(solution)/shard_map/reduce_sum | solution.py:65
  377.9 0.0 copy-done.1
  377.9 0.1 fusion.7
  378.0 12.9 %collective-permute-start = (bf16[1,64,3584]{2,1,0:T(8,128)(2,1)S(1)}, bf16[1,64,3584]{2,1,0:T(8,128)(2,1)S(1)}, u32[]{:S(2)}, u32[]{:S(2)}) collective-permute-start(bf16[1,64,3584]{2,1,0:T(8,128)(2,1)S(1)} %fusion.7), channel_id=1, source_target_pairs={{0,64},{64,128},{128,192},{192,256},{256,320},{320,384},{384,448},... | collective-permute-start | bytes 1376264 | tf_op jit(solution)/shard_map/ppermute | solution.py:11
  390.9 14.7 %collective-permute-done = bf16[1,64,3584]{2,1,0:T(8,128)(2,1)S(1)} collective-permute-done((bf16[1,64,3584]{2,1,0:T(8,128)(2,1)S(1)}, bf16[1,64,3584]{2,1,0:T(8,128)(2,1)S(1)}, u32[]{:S(2)}, u32[]{:S(2)}) %collective-permute-start) | collective-permute-done | bytes 458784 | tf_op jit(solution)/shard_map/ppermute | solution.py:11
  405.6 0.8 copy.14
  (11 shorter events, 0.0 us)
Async XLA Ops:
  0.0 185.3 %copy-start = (bf16[1,1,3584,256]{3,2,1,0:T(8,128)(2,1)S(1)}, bf16[1,1,3584,256]{3,2,1,0:T(8,128)(2,1)}, u32[]{:S(2)}) copy-start(bf16[1,1,3584,256]{3,2,1,0:T(8,128)(2,1)} %param.10) | copy-start | bytes 5505028
  185.3 2.1 copy-start.2
  192.4 6.0 %copy-start.3 = (s32[1,64,2]{1,2,0:T(2,128)S(1)}, s32[1,64,2]{1,2,0:T(2,128)}, u32[]{:S(2)}) copy-start(s32[1,64,2]{1,2,0:T(2,128)} %param.8) | copy-start | bytes 1540
  192.4 6.3 %copy-start.4 = (f32[1,64,2]{1,2,0:T(2,128)S(1)}, f32[1,64,2]{1,2,0:T(2,128)}, u32[]{:S(2)}) copy-start(f32[1,64,2]{1,2,0:T(2,128)} %param.9) | copy-start | bytes 1540
  192.4 167.6 %all-to-all-start.1 = ((bf16[64,16,3584]{2,1,0:T(8,128)(2,1)}), bf16[64,16,3584]{2,1,0:T(8,128)(2,1)}, u32[]{:S(2)}, u32[]{:S(2)}) async-start(bf16[64,16,3584]{2,1,0:T(8,128)(2,1)} %bitcast.38), calls=%async_computation.1 | async-start | bytes 14680064 | tf_op jit(solution)/shard_map/all_to_all | solution.py:54
  373.7 4.1 %copy-start.1 = (bf16[1,64,3584]{2,1,0:T(8,128)(2,1)S(1)}, bf16[1,64,3584]{2,1,0:T(8,128)(2,1)}, u32[]{:S(2)}) copy-start(bf16[1,64,3584]{2,1,0:T(8,128)(2,1)} %param.6) | copy-start | bytes 1376260
  378.0 27.6 %collective-permute-start = (bf16[1,64,3584]{2,1,0:T(8,128)(2,1)S(1)}, bf16[1,64,3584]{2,1,0:T(8,128)(2,1)S(1)}, u32[]{:S(2)}, u32[]{:S(2)}) collective-permute-start(bf16[1,64,3584]{2,1,0:T(8,128)(2,1)S(1)} %fusion.7), channel_id=1, source_target_pairs={{0,64},{64,128},{128,192},{192,256},{256,320},{320,384},{384,448},... | collective-permute-start | bytes 1376264 | tf_op jit(solution)/shard_map/ppermute | solution.py:11
where the time goes:
time: 410 us; the launch traced here: 406 us
  waiting for transfers between devices  176 us (43%)
  blocking collectives  175 us (43%)
  starting transfers between devices  19 us (5%)
  local copies, waits for them, and re-layouts  14.9 us (4%)
  other arithmetic  13.6 us (3%)
  matrix products  7.55 us (2%)
    all_to_all x1, blocking collectives, routed_part(): lax.all_to_all(outgoing, 'expert', split_axis=0, concat_axis=0, tiled=True)  175 us
    all_to_all x1, waiting for transfers between devices, routed_part(): lax.all_to_all(partial_value.reshape(owners, slots, width), 'expert', spl...  161 us
    ppermute x1, waiting for transfers between devices, passed_along(): return lax.ppermute(x, axis, [(i, (i + by) % size) for i in range(size)])  14.7 us
    ppermute x1, starting transfers between devices, passed_along(): return lax.ppermute(x, axis, [(i, (i + by) % size) for i in range(size)])  12.9 us
  transfers between devices with their start and end apart: 2, of which 2 were waited for; matrix products, arithmetic and copies ran while one was open for 0% of the time, Pallas kernels for 0%

commit v1 on v0

v1 whole, which is shorter than its diff:
```python
import functools

import jax
import jax.numpy as jnp
from jax import lax
from jax.experimental import pallas as pl
from jax.experimental.pallas import tpu as pltpu
from jax.sharding import PartitionSpec as P

EXPERTS = 8
SHARDS = 8
PLANES = 4
SECTIONS = 8
COLUMN_PARTS = 2
TILE = 512
MESH = pl.DeviceIdType.MESH
BF16 = jnp.bfloat16
F32 = jnp.float32


def layer_kernel(
    hidden,
    gain,
    routes,
    gates,
    w_gate_up,
    w_down,
    out,
    raw,
    meta,
    sorted_rows,
    rows,
    gate_up_w,
    down_w,
    act,
    piece,
    back,
    part,
    home,
    layer_out,
    own_w_sem,
    w_send,
    w_recv,
    raw_send,
    raw_recv,
    meta_send,
    meta_recv,
    go_send,
    go_recv,
    back_send,
    back_recv,
    part_send,
    part_recv,
    hand_send,
    hand_recv,
):
    tokens, width = hidden.shape
    cap = rows.shape[2]
    inner = w_down.shape[0]
    slots = EXPERTS * cap
    span = width // COLUMN_PARTS

    section = lax.axis_index("section")
    me = lax.axis_index("expert")
    z = lax.rem(me, PLANES)
    column = lax.div(me, PLANES)
    y = lax.rem(column, 4)
    rank = lax.div(me, SHARDS)
    y_half, y_odd = lax.div(y, 2), lax.rem(y, 2)
    side = lax.rem(y_half + y_odd, 2)
    partner = (column - y_odd + 1 - y_odd) * PLANES + z
    after = lax.rem(section + 1, SECTIONS)
    before = lax.rem(section + SECTIONS - 1, SECTIONS)

    def in_plane(e):
        half = lax.rem(e, 2)
        return (lax.div(e, 2) * 4 + 2 * half + lax.rem(half + side, 2)) * PLANES + z

    def along_z(plane):
        return column * PLANES + plane

    def remote(src, dst, send, recv, to, to_section=None):
        return pltpu.make_async_remote_copy(
            src_ref=src,
            dst_ref=dst,
            send_sem=send,
            recv_sem=recv,
            device_id=(section if to_section is None else to_section, to),
            device_id_type=MESH,
        )

    own_gate_up = pltpu.make_async_copy(w_gate_up, gate_up_w.at[0], own_w_sem.at[0])
    own_down = pltpu.make_async_copy(w_down, down_w.at[pl.ds(0, inner)], own_w_sem.at[1])
    own_gate_up.start()
    own_down.start()

    barrier = pltpu.get_barrier_semaphore()

    def greet(to, to_section):
        pl.semaphore_signal(barrier, inc=1, device_id=(to_section, to), device_id_type=MESH)

    for i in range(1, PLANES):
        greet(along_z(lax.rem(z + i, PLANES)), section)
    for d in range(1, EXPERTS):
        greet(in_plane(lax.rem(rank + d, EXPERTS)), section)
    greet(partner, section)
    greet(me, after)
    greet(me, before)
    pl.semaphore_wait(barrier, PLANES - 1 + EXPERTS - 1 + 3)

    send_gate_up = remote(w_gate_up, gate_up_w.at[1], w_send.at[0], w_recv.at[0], partner)
    send_gate_up.start()
    send_down = remote(w_down, down_w.at[pl.ds(inner, inner)], w_send.at[1], w_recv.at[1], partner)
    send_down.start()

    rows_f32 = hidden[...].astype(F32)
    scale = lax.rsqrt(jnp.mean(rows_f32 * rows_f32, axis=1, keepdims=True) + 1e-06)
    raw[z] = (rows_f32 * scale * gain[...]).astype(BF16)

    lane = lax.broadcasted_iota(jnp.int32, (tokens, slots), 1)
    token = lax.broadcasted_iota(jnp.int32, (tokens, slots), 0)
    first, second = routes[:, 0:1], routes[:, 1:2]
    names_first, names_second = lane == first, lane == second
    one_hot = (jnp.where(names_first, 1.0, 0.0) + jnp.where(names_second, 1.0, 0.0)).astype(BF16)
    below = jnp.where(
        lax.broadcasted_iota(jnp.int32, (tokens, tokens), 0)
        > lax.broadcasted_iota(jnp.int32, (tokens, tokens), 1),
        1.0,
        0.0,
    ).astype(BF16)
    earlier = jnp.dot(below, one_hot, preferred_element_type=F32)
    place_first = first.astype(F32) * cap + jnp.sum(
        jnp.where(names_first, earlier, 0.0), axis=1, keepdims=True
    )
    place_second = second.astype(F32) * cap + jnp.sum(
        jnp.where(names_second, earlier, 0.0), axis=1, keepdims=True
    )
    lane_f32, token_f32 = lane.astype(F32), token.astype(F32)
    at_first, at_second = lane_f32 == place_first, lane_f32 == place_second
    slot_token = jnp.sum(
        jnp.where(at_first, token_f32, 0.0) + jnp.where(at_second, token_f32, 0.0),
        axis=0,
        keepdims=True,
    )
    slot_gate = jnp.sum(
        jnp.where(at_first, gates[:, 0:1], 0.0) + jnp.where(at_second, gates[:, 1:2], 0.0),
        axis=0,
        keepdims=True,
    )
    meta_row = lax.broadcasted_iota(jnp.int32, (8, slots), 0)
    meta[z] = jnp.where(meta_row == 0, slot_token, slot_gate)

    for i in range(1, PLANES):
        to = lax.rem(z + i, PLANES)
        remote(meta.at[z], meta.at[z], meta_send.at[to], meta_recv.at[z], along_z(to)).start()
        remote(raw.at[z], raw.at[z], raw_send.at[to], raw_recv.at[z], along_z(to)).start()

    def sort_and_send(i, plane):
        placed = jnp.where(token_f32 == meta[plane, 0:1, :], 1.0, 0.0).astype(BF16)
        for c in range(0, width, TILE):
            block = lax.dot_general(
                placed,
                raw[plane, :, c : c + TILE],
                (((0,), (0,)), ((), ())),
                preferred_element_type=F32,
            ).astype(BF16)
            sorted_rows[plane, :, :, c : c + TILE] = block.reshape(EXPERTS, cap, TILE)
        for d in range(1, EXPERTS):
            e = lax.rem(rank + d, EXPERTS)
            remote(
                sorted_rows.at[plane, e],
                rows.at[plane, rank],
                go_send.at[plane * EXPERTS + e],
                go_recv.at[plane * EXPERTS + rank],
                in_plane(e),
            ).start()
        rows[plane, rank] = sorted_rows[plane, rank]

    def dispatch(i, carry):
        plane = lax.rem(z + i, PLANES)
        from_z = along_z(plane)
        remote(meta.at[z], meta.at[plane], meta_send.at[plane], meta_recv.at[plane], from_z).wait_recv()
        remote(raw.at[z], raw.at[plane], raw_send.at[plane], raw_recv.at[plane], from_z).wait_recv()
        sort_and_send(i, plane)
        return carry

    sort_and_send(0, z)
    lax.fori_loop(1, PLANES, dispatch, 0)

    own_gate_up.wait()
    own_down.wait()

    def activated(plane, shard):
        gate_up = jnp.dot(
            rows[plane].reshape(slots, width), gate_up_w[shard], preferred_element_type=F32
        )
        gate, up = gate_up[:, :inner], gate_up[:, inner:]
        act[plane, :, shard * inner : (shard + 1) * inner] = (
            gate / (1.0 + jnp.exp(-gate)) * up
        ).astype(BF16)

    def own_shard(i, carry):
        plane = lax.rem(z + i, PLANES)
        for d in range(1, EXPERTS):
            e = lax.rem(rank + d, EXPERTS)
            remote(
                sorted_rows.at[plane, e],
                rows.at[plane, e],
                go_send.at[plane * EXPERTS + e],
                go_recv.at[plane * EXPERTS + e],
                in_plane(e),
            ).wait_recv()
        activated(plane, 0)
        return carry

    lax.fori_loop(0, PLANES, own_shard, 0)
    send_gate_up.wait_recv()

    def other_shard(i, carry):
        activated(lax.rem(z + i, PLANES), 1)
        return carry

    lax.fori_loop(0, PLANES, other_shard, 0)
    send_down.wait_recv()

    def cols(h):
        return pl.ds(h * span, span)

    def back_copy(plane, e, h, mine):
        return remote(
            piece.at[plane, e, :, cols(h)],
            back.at[plane, rank if mine else e, :, cols(h)],
            back_send.at[(h * PLANES + plane) * EXPERTS + e],
            back_recv.at[(h * PLANES + plane) * EXPERTS + (rank if mine else e)],
            in_plane(e),
        )

    for h in range(COLUMN_PARTS):

        def down(i, carry, h=h):
            plane = lax.rem(z + i, PLANES)
            block = jnp.dot(
                act[plane], down_w[:, h * span : (h + 1) * span], preferred_element_type=F32
            ).astype(BF16)
            piece[plane, :, :, h * span : (h + 1) * span] = block.reshape(EXPERTS, cap, span)
            for d in range(1, EXPERTS):
                back_copy(plane, lax.rem(rank + d, EXPERTS), h, True).start()
            back[plane, rank, :, h * span : (h + 1) * span] = piece[
                plane, rank, :, h * span : (h + 1) * span
            ]
            return carry

        lax.fori_loop(0, PLANES, down, 0)

    def part_copy(plane, h, mine):
        return remote(
            part.at[plane, :, cols(h)],
            home.at[z if mine else plane, :, cols(h)],
            part_send.at[h * PLANES + plane],
            part_recv.at[h * PLANES + (z if mine else plane)],
            along_z(plane),
        )

    def combined(plane, h):
        weight = jnp.where(token_f32 == meta[plane, 0:1, :], meta[plane, 1:2, :], 0.0)
        high = weight.astype(BF16)
        low = (weight - high.astype(F32)).astype(BF16)
        arrived = back[plane, :, :, h * span : (h + 1) * span].reshape(slots, span)
        return (
            jnp.dot(high, arrived, preferred_element_type=F32)
            + jnp.dot(low, arrived, preferred_element_type=F32)
        ).astype(BF16)

    def wait_back(plane, h):
        for d in range(1, EXPERTS):
            back_copy(plane, lax.rem(rank + d, EXPERTS), h, False).wait_recv()

    def hand_copy(h):
        return remote(
            layer_out.at[:, cols(h)],
            out.at[:, cols(h)],
            hand_send.at[h],
            hand_recv.at[h],
            me,
            after,
        )

    for h in range(COLUMN_PARTS):
        lo, hi = h * span, (h + 1) * span

        def combine(i, carry, h=h, lo=lo, hi=hi):
            plane = lax.rem(z + i, PLANES)
            wait_back(plane, h)
            part[plane, :, lo:hi] = combined(plane, h)
            part_copy(plane, h, True).start()
            return carry

        lax.fori_loop(1, PLANES, combine, 0)
        wait_back(z, h)
        home[z, :, lo:hi] = combined(z, h)

    for h in range(COLUMN_PARTS):
        lo, hi = h * span, (h + 1) * span
        for i in range(1, PLANES):
            part_copy(lax.rem(z + i, PLANES), h, False).wait_recv()
        total = home[0, :, lo:hi].astype(F32)
        for p in range(1, PLANES):
            total = total + home[p, :, lo:hi].astype(F32)
        layer_out[:, lo:hi] = (hidden[:, lo:hi].astype(F32) + total).astype(BF16)
        hand_copy(h).start()

    send_gate_up.wait_send()
    send_down.wait_send()

    def sent(i, carry):
        plane = lax.rem(z + i, PLANES)
        for d in range(1, EXPERTS):
            e = lax.rem(rank + d, EXPERTS)
            remote(
                sorted_rows.at[plane, e],
                rows.at[plane, rank],
                go_send.at[plane * EXPERTS + e],
                go_recv.at[plane * EXPERTS + rank],
                in_plane(e),
            ).wait_send()
            for h in range(COLUMN_PARTS):
                back_copy(plane, e, h, True).wait_send()
        return carry

    lax.fori_loop(0, PLANES, sent, 0)
    for i in range(1, PLANES):
        to = lax.rem(z + i, PLANES)
        remote(meta.at[z], meta.at[z], meta_send.at[to], meta_recv.at[z], along_z(to)).wait_send()
        remote(raw.at[z], raw.at[z], raw_send.at[to], raw_recv.at[z], along_z(to)).wait_send()
        for h in range(COLUMN_PARTS):
            part_copy(to, h, True).wait_send()
    for h in range(COLUMN_PARTS):
        hand_copy(h).wait()


def local(hidden_rows, norm_gain, routes, gates, w_gate_up, w_down):
    hidden = hidden_rows[0]
    tokens, width = hidden.shape
    picks = routes.shape[2]
    cap = tokens * picks // EXPERTS
    inner = w_down.shape[2]
    vmem = pl.BlockSpec(memory_space=pltpu.VMEM)
    anywhere = pl.BlockSpec(memory_space=pl.ANY)
    dma = pltpu.SemaphoreType.DMA
    blocks = pltpu.VMEM((PLANES, EXPERTS, cap, width), BF16)
    per_plane = pltpu.VMEM((PLANES, tokens, width), BF16)
    handoff = pl.pallas_call(
        layer_kernel,
        out_shape=jax.ShapeDtypeStruct((tokens, width), BF16),
        in_specs=[vmem] * 4 + [anywhere] * 2,
        out_specs=anywhere,
        scratch_shapes=[
            per_plane,
            pltpu.VMEM((PLANES, 8, EXPERTS * cap), F32),
            blocks,
            blocks,
            pltpu.VMEM((2, width, 2 * inner), BF16),
            pltpu.VMEM((2 * inner, width), BF16),
            pltpu.VMEM((PLANES, EXPERTS * cap, 2 * inner), BF16),
            blocks,
            blocks,
            per_plane,
            per_plane,
            pltpu.VMEM((tokens, width), BF16),
            dma((2,)),
            dma((2,)),
            dma((2,)),
            dma((PLANES,)),
            dma((PLANES,)),
            dma((PLANES,)),
            dma((PLANES,)),
            dma((PLANES * EXPERTS,)),
            dma((PLANES * EXPERTS,)),
            dma((COLUMN_PARTS * PLANES * EXPERTS,)),
            dma((COLUMN_PARTS * PLANES * EXPERTS,)),
            dma((COLUMN_PARTS * PLANES,)),
            dma((COLUMN_PARTS * PLANES,)),
            dma((COLUMN_PARTS,)),
            dma((COLUMN_PARTS,)),
        ],
        compiler_params=pltpu.CompilerParams(
            collective_id=0, has_side_effects=True, vmem_limit_bytes=48 * 1024 * 1024
        ),
        cost_estimate=pl.CostEstimate(
            flops=6 * EXPERTS * SHARDS * cap * width * inner,
            bytes_accessed=2 * (tokens * width * 2 + 3 * width * inner),
            transcendentals=EXPERTS * SHARDS * cap * inner,
        ),
    )(hidden, norm_gain, routes[0], gates[0], w_gate_up[0, 0], w_down[0, 0])
    return handoff[None]


def solution(mesh):
    in_specs = (
        P("section", "expert", None),
        P("section", None),
        P("section", "expert", None),
        P("section", "expert", None),
        P("section", "expert", None, None),
        P("section", "expert", None, None),
    )
    out_specs = P("section", "expert", None)
    return jax.shard_map(local, mesh=mesh, in_specs=in_specs, out_specs=out_specs, check_vma=False)
```

time: 410 us -> 165 us (0.40)
  the two profiles are of different devices: /device:TPU:1 before, /device:TPU:38 now
where the time goes in v1:
time: 165 us; the launch traced here: 164 us
  Pallas kernels  158 us (96%)
  local copies, waits for them, and re-layouts  6.71 us (4%)
    pallas_call x1, Pallas kernels, local(): pl.pallas_call(layer_kernel, out_shape=jax.ShapeDtypeStruct((tokens, widt...  158 us
    unnamed x9, local copies, waits for them, and re-layouts  5.18 us

profile of v1, /device:TPU:38, one launch (start us, length us, event | category | flops | bytes accessed | tf_op | source)
XLA Modules:
  0.0 164.2 jit_solution(11493496485332414863)
XLA Ops:
  0.0 0.8 copy.7.routes
  0.8 0.8 copy.8.gates
  1.5 0.0 copy-start
  1.5 1.5 copy-done
  3.0 0.0 copy-start.1
  3.0 1.2 copy-done.1
  4.2 0.0 copy-start.2
  4.2 1.0 copy-done.2
  5.2 0.0 copy-start.3
  5.2 0.7 copy-done.3
  5.9 157.5 %shard_map.64 = bf16[64,3584]{1,0:T(8,128)(2,1)S(1)} custom-call(bf16[64,3584]{1,0:T(8,128)(2,1)S(1)} %bitcast.9, f32[1,3584]{1,0:T(1,128)S(1)} %copy-done.3, s32[64,2]{1,0:T(8,128)S(1)} %copy.7.routes, f32[64,2]{1,0:T(8,128)S(1)} %copy.8.gates, bf16[3584,256]{1,0:T(8,128)(2,1)S(1)} %bitcast.7, bf16[128,3584]{1,0:T(8,128)(2,1)S(1)} %bitcast.8), custom_call_target="tpu_custom_call" | custom-call | flops 2818572288 | bytes 3670016 | tf_op jit(solution)/shard_map/pallas_call | solution.py:352
  163.5 0.8 copy.10
Async XLA Ops:
  1.5 1.5 copy-start
  3.0 1.2 copy-start.1
  4.2 1.0 copy-start.2
  5.2 0.7 copy-start.3

commit v2 on v0

v2 whole, which is shorter than its diff:
```python
import jax
import jax.numpy as jnp
from jax import lax
from jax.experimental import pallas as pl
from jax.experimental.pallas import tpu as pltpu
from jax.sharding import PartitionSpec as P

EXPERTS = 8
SHARDS = 8
PLANES = 4
SECTIONS = 8
PIECES = 4
MESH = pl.DeviceIdType.MESH
BF16 = jnp.bfloat16
F32 = jnp.float32


def layer_kernel(
    hidden_hbm,
    gain_hbm,
    routes_hbm,
    gates_hbm,
    w_gate_up,
    w_down,
    out,
    hidden,
    gain,
    routes,
    gates,
    raw,
    meta,
    sorted_rows,
    rows,
    gate_up_w,
    down_w,
    total_gate_up,
    act,
    piece,
    back,
    part,
    home,
    layer_out,
    in_sem,
    gu_send,
    gu_recv,
    wd_send,
    wd_recv,
    up_send,
    dn_send,
    raw_recv,
    meta_send,
    meta_recv,
    go_send,
    go_recv,
    back_send,
    back_recv,
    part_send,
    part_recv,
    hand_send,
    hand_recv,
):
    tokens, width = hidden.shape
    cap = rows.shape[3]
    inner = w_down.shape[0]
    slots = EXPERTS * cap
    span = width // PIECES

    section = lax.axis_index("section")
    me = lax.axis_index("expert")
    z = lax.rem(me, PLANES)
    column = lax.div(me, PLANES)
    y = lax.rem(column, 4)
    rank = lax.div(me, SHARDS)
    y_half, y_odd = lax.div(y, 2), lax.rem(y, 2)
    side = lax.rem(y_half + y_odd, 2)
    partner = (column - y_odd + 1 - y_odd) * PLANES + z
    after = lax.rem(section + 1, SECTIONS)
    before = lax.rem(section + SECTIONS - 1, SECTIONS)
    flip = lax.div(z, 2)
    z_low = z + flip * (PLANES - 1 - 2 * z)

    def in_plane(e):
        half = lax.rem(e, 2)
        return (lax.div(e, 2) * 4 + 2 * half + lax.rem(half + side, 2)) * PLANES + z

    def along_z(plane):
        return column * PLANES + plane

    def other_plane(i):
        low = jnp.where(i - 1 < z_low, i - 1, i)
        return low + flip * (PLANES - 1 - 2 * low)

    def cols(c):
        return pl.ds(pl.multiple_of(c * span, span), span)

    def remote(src, dst, send, recv, to, to_section=None):
        return pltpu.make_async_remote_copy(
            src_ref=src,
            dst_ref=dst,
            send_sem=send,
            recv_sem=recv,
            device_id=(section if to_section is None else to_section, to),
            device_id_type=MESH,
        )

    barrier = pltpu.get_barrier_semaphore()

    def greet(to, to_section):
        pl.semaphore_signal(barrier, inc=1, device_id=(to_section, to), device_id_type=MESH)

    for i in range(1, PLANES):
        greet(along_z(lax.rem(z + i, PLANES)), section)
    for d in range(1, EXPERTS):
        greet(in_plane(lax.rem(rank + d, EXPERTS)), section)
    greet(partner, section)
    greet(me, after)
    greet(me, before)

    own_copies = [
        pltpu.make_async_copy(hidden_hbm, hidden, in_sem.at[0]),
        pltpu.make_async_copy(gain_hbm, gain, in_sem.at[1]),
        pltpu.make_async_copy(routes_hbm, routes, in_sem.at[2]),
        pltpu.make_async_copy(gates_hbm, gates, in_sem.at[3]),
        pltpu.make_async_copy(w_gate_up, gate_up_w.at[0], in_sem.at[4]),
    ]
    for copy in own_copies:
        copy.start()

    def own_down(c):
        return pltpu.make_async_copy(
            w_down.at[:, cols(c)], down_w.at[c, pl.ds(0, inner)], in_sem.at[5 + c]
        )

    for c in range(PIECES):
        own_down(c).start()
    for copy in own_copies[:4]:
        copy.wait()

    rows_f32 = hidden[...].astype(F32)
    scale = lax.rsqrt(jnp.mean(rows_f32 * rows_f32, axis=1, keepdims=True) + 1e-06)
    for c in range(PIECES):
        lo, hi = c * span, (c + 1) * span
        raw[c, z] = (hidden[:, lo:hi].astype(F32) * scale * gain[:, lo:hi]).astype(BF16)

    names = lax.broadcasted_iota(jnp.int32, (16, tokens), 0)
    first, second = routes[0:1, :], routes[1:2, :]
    names_first, names_second = names == first, names == second
    one_hot = (jnp.where(names_first, 1.0, 0.0) + jnp.where(names_second, 1.0, 0.0)).astype(BF16)
    above = jnp.where(
        lax.broadcasted_iota(jnp.int32, (tokens, tokens), 0)
        < lax.broadcasted_iota(jnp.int32, (tokens, tokens), 1),
        1.0,
        0.0,
    ).astype(BF16)
    earlier = jnp.dot(one_hot, above, preferred_element_type=F32)
    slot_first = first.astype(F32) * cap + jnp.sum(
        jnp.where(names_first, earlier, 0.0), axis=0, keepdims=True
    )
    slot_second = second.astype(F32) * cap + jnp.sum(
        jnp.where(names_second, earlier, 0.0), axis=0, keepdims=True
    )
    meta_row = lax.broadcasted_iota(jnp.int32, (8, tokens), 0)
    meta[z, :, 0:tokens] = jnp.where(
        meta_row == 0,
        slot_first,
        jnp.where(
            meta_row == 1, slot_second, jnp.where(meta_row == 2, gates[0:1, :], gates[1:2, :])
        ),
    )
    meta[z, :, tokens : 2 * tokens] = jnp.zeros((8, tokens), F32)

    pl.semaphore_wait(barrier, PLANES - 1 + EXPERTS - 1 + 3)

    def gate_up_copy(c):
        return remote(
            w_gate_up.at[pl.ds(pl.multiple_of(c * span, span), span)],
            gate_up_w.at[1, pl.ds(pl.multiple_of(c * span, span), span)],
            gu_send.at[c],
            gu_recv.at[c],
            partner,
        )

    def down_copy(c):
        return remote(
            w_down.at[:, cols(c)],
            down_w.at[c, pl.ds(inner, inner)],
            wd_send.at[c],
            wd_recv.at[c],
            partner,
        )

    def meta_copy(to, plane):
        return remote(
            meta.at[plane], meta.at[plane], meta_send.at[to], meta_recv.at[plane], along_z(to)
        )

    def up_copy(c, plane):
        at = c * PLANES + plane
        return remote(raw.at[c, plane], raw.at[c, plane], up_send.at[at], raw_recv.at[at], me + 1)

    def dn_copy(c, plane):
        at = c * PLANES + plane
        return remote(raw.at[c, plane], raw.at[c, plane], dn_send.at[at], raw_recv.at[at], me - 1)

    def pass_on(c, plane, act_on):
        @pl.when((plane <= z) & (z < PLANES - 1))
        def _():
            act_on(up_copy(c, plane))

        @pl.when((plane >= z) & (z > 0))
        def _():
            act_on(dn_copy(c, plane))

    def go_copy(c, plane, e, mine):
        slot = rank if mine else e
        at = (c * PLANES + plane) * EXPERTS
        return remote(
            sorted_rows.at[c, plane, e],
            rows.at[c, plane, slot],
            go_send.at[at + e],
            go_recv.at[at + slot],
            in_plane(e),
        )

    slot_row = lax.broadcasted_iota(jnp.int32, (slots, tokens), 0).astype(F32)

    def sort_and_send(c, plane):
        placed = (
            jnp.where(slot_row == meta[plane, 0:1, 0:tokens], 1.0, 0.0)
            + jnp.where(slot_row == meta[plane, 1:2, 0:tokens], 1.0, 0.0)
        ).astype(BF16)
        block = jnp.dot(placed, raw[c, plane], preferred_element_type=F32).astype(BF16)
        sorted_rows[c, plane] = block.reshape(EXPERTS, cap, span)
        for d in range(1, EXPERTS):
            go_copy(c, plane, lax.rem(rank + d, EXPERTS), True).start()
        rows[c, plane, rank] = sorted_rows[c, plane, rank]

    for i in range(1, PLANES):
        meta_copy(lax.rem(z + i, PLANES), z).start()
    for c in range(PIECES):
        pass_on(c, z, lambda copy: copy.start())
        gate_up_copy(c).start()

    def own_dispatch(c, carry):
        sort_and_send(c, z)
        return carry

    lax.fori_loop(0, PIECES, own_dispatch, 0)
    for i in range(1, PLANES):
        plane = lax.rem(z + i, PLANES)
        meta_copy(z, plane).wait_recv()

    def dispatch(n, carry):
        c = lax.div(n, PLANES - 1)
        plane = other_plane(lax.rem(n, PLANES - 1) + 1)
        at = c * PLANES + plane
        remote(raw.at[c, plane], raw.at[c, plane], up_send.at[at], raw_recv.at[at], me).wait_recv()
        pass_on(c, plane, lambda copy: copy.start())
        sort_and_send(c, plane)
        return carry

    lax.fori_loop(0, PIECES * (PLANES - 1), dispatch, 0)
    for c in range(PIECES):
        down_copy(c).start()

    own_copies[4].wait()

    def gate_up(c, carry):
        def arrived(plane, carry):
            for d in range(1, EXPERTS):
                go_copy(c, plane, lax.rem(rank + d, EXPERTS), False).wait_recv()
            return carry

        lax.fori_loop(0, PLANES, arrived, 0)
        gate_up_copy(c).wait_recv()
        block = rows[c].reshape(PLANES * slots, span)
        for s in range(2):
            w = gate_up_w[s, pl.ds(pl.multiple_of(c * span, span), span), :]
            total_gate_up[s] = total_gate_up[s] + jnp.dot(block, w, preferred_element_type=F32)
        return carry

    total_gate_up[...] = jnp.zeros_like(total_gate_up)
    lax.fori_loop(0, PIECES, gate_up, 0)
    for s in range(2):
        gate = total_gate_up[s, :, 0:inner]
        act[:, s * inner : (s + 1) * inner] = (
            gate / (1.0 + jnp.exp(-gate)) * total_gate_up[s, :, inner : 2 * inner]
        ).astype(BF16)

    def back_copy(c, plane, e, mine):
        slot = rank if mine else e
        at = (c * PLANES + plane) * EXPERTS
        return remote(
            piece.at[c, plane, e],
            back.at[c, plane, slot],
            back_send.at[at + e],
            back_recv.at[at + slot],
            in_plane(e),
        )

    def down(c, carry):
        own_down(c).wait()
        down_copy(c).wait_recv()
        block = jnp.dot(act[...], down_w[c], preferred_element_type=F32).astype(BF16)
        piece[c] = block.reshape(PLANES, EXPERTS, cap, span)

        def send(i, carry):
            plane = jnp.where(i == PLANES, z, other_plane(PLANES - i))
            for d in range(1, EXPERTS):
                back_copy(c, plane, lax.rem(rank + d, EXPERTS), True).start()
            back[c, plane, rank] = piece[c, plane, rank]
            return carry

        lax.fori_loop(1, PLANES + 1, send, 0)
        return carry

    lax.fori_loop(0, PIECES, down, 0)

    def part_copy(c, plane, mine):
        slot = z if mine else plane
        return remote(
            part.at[c, plane],
            home.at[c, slot],
            part_send.at[c * PLANES + plane],
            part_recv.at[c * PLANES + slot],
            along_z(plane),
        )

    def combined(c, plane):
        for d in range(1, EXPERTS):
            back_copy(c, plane, lax.rem(rank + d, EXPERTS), False).wait_recv()
        weight = jnp.where(
            slot_row == meta[plane, 0:1, 0:tokens], meta[plane, 2:3, 0:tokens], 0.0
        ) + jnp.where(slot_row == meta[plane, 1:2, 0:tokens], meta[plane, 3:4, 0:tokens], 0.0)
        high = weight.astype(BF16)
        low = (weight - high.astype(F32)).astype(BF16)
        both = lax.dot_general(
            jnp.concatenate([high, low], axis=1),
            back[c, plane].reshape(slots, span),
            (((0,), (0,)), ((), ())),
            preferred_element_type=F32,
        )
        return (both[0:tokens] + both[tokens : 2 * tokens]).astype(BF16)

    def hand_copy(c):
        return remote(
            layer_out.at[c], out.at[:, cols(c)], hand_send.at[c], hand_recv.at[c], me, after
        )

    def combine(c):
        def send(i, carry):
            plane = other_plane(PLANES - i)
            part[c, plane] = combined(c, plane)
            part_copy(c, plane, True).start()
            return carry

        lax.fori_loop(1, PLANES, send, 0)
        home[c, z] = combined(c, z)

    def finish(c):
        for i in range(1, PLANES):
            part_copy(c, lax.rem(z + i, PLANES), False).wait_recv()
        total = home[c, 0].astype(F32)
        for p in range(1, PLANES):
            total = total + home[c, p].astype(F32)
        layer_out[c] = (hidden[:, cols(c)].astype(F32) + total).astype(BF16)
        hand_copy(c).start()

    def combine_and_finish(c, carry):
        combine(c)
        finish(c - 1)
        return carry

    combine(0)
    lax.fori_loop(1, PIECES, combine_and_finish, 0)
    finish(PIECES - 1)

    def sent(c, carry):
        gate_up_copy(c).wait_send()
        down_copy(c).wait_send()

        def sent_plane(plane, carry):
            for d in range(1, EXPERTS):
                e = lax.rem(rank + d, EXPERTS)
                go_copy(c, plane, e, True).wait_send()
                back_copy(c, plane, e, True).wait_send()
            pass_on(c, plane, lambda copy: copy.wait_send())
            return carry

        lax.fori_loop(0, PLANES, sent_plane, 0)
        for i in range(1, PLANES):
            part_copy(c, lax.rem(z + i, PLANES), True).wait_send()
        return carry

    lax.fori_loop(0, PIECES, sent, 0)
    for i in range(1, PLANES):
        meta_copy(lax.rem(z + i, PLANES), z).wait_send()
    for c in range(PIECES):
        hand_copy(c).wait()


def local(hidden_rows, norm_gain, routes, gates, w_gate_up, w_down):
    hidden = hidden_rows[0]
    tokens, width = hidden.shape
    picks = routes.shape[2]
    cap = tokens * picks // EXPERTS
    inner = w_down.shape[2]
    span = width // PIECES
    slots = EXPERTS * cap
    hbm = pl.BlockSpec(memory_space=pltpu.HBM)
    dma = pltpu.SemaphoreType.DMA
    blocks = pltpu.VMEM((PIECES, PLANES, EXPERTS, cap, span), BF16)
    per_plane = pltpu.VMEM((PIECES, PLANES, tokens, span), BF16)
    handoff = pl.pallas_call(
        layer_kernel,
        out_shape=jax.ShapeDtypeStruct((tokens, width), BF16),
        in_specs=[hbm] * 6,
        out_specs=hbm,
        scratch_shapes=[
            pltpu.VMEM((tokens, width), BF16),
            pltpu.VMEM((1, width), F32),
            pltpu.VMEM((picks, tokens), jnp.int32),
            pltpu.VMEM((picks, tokens), F32),
            per_plane,
            pltpu.VMEM((PLANES, 8, 2 * tokens), F32),
            blocks,
            blocks,
            pltpu.VMEM((2, width, 2 * inner), BF16),
            pltpu.VMEM((PIECES, 2 * inner, span), BF16),
            pltpu.VMEM((2, PLANES * slots, 2 * inner), F32),
            pltpu.VMEM((PLANES * slots, 2 * inner), BF16),
            blocks,
            blocks,
            per_plane,
            per_plane,
            pltpu.VMEM((PIECES, tokens, span), BF16),
            dma((5 + PIECES,)),
            dma((PIECES,)),
            dma((PIECES,)),
            dma((PIECES,)),
            dma((PIECES,)),
            dma((PIECES * PLANES,)),
            dma((PIECES * PLANES,)),
            dma((PIECES * PLANES,)),
            dma((PLANES,)),
            dma((PLANES,)),
            dma((PIECES * PLANES * EXPERTS,)),
            dma((PIECES * PLANES * EXPERTS,)),
            dma((PIECES * PLANES * EXPERTS,)),
            dma((PIECES * PLANES * EXPERTS,)),
            dma((PIECES * PLANES,)),
            dma((PIECES * PLANES,)),
            dma((PIECES,)),
            dma((PIECES,)),
        ],
        compiler_params=pltpu.CompilerParams(
            collective_id=0, has_side_effects=True, vmem_limit_bytes=62 * 1024 * 1024
        ),
        cost_estimate=pl.CostEstimate(
            flops=6 * EXPERTS * SHARDS * cap * width * inner,
            bytes_accessed=2 * (tokens * width * 2 + 3 * width * inner),
            transcendentals=EXPERTS * SHARDS * cap * inner,
        ),
    )(hidden, norm_gain, routes[0].T, gates[0].T, w_gate_up[0, 0], w_down[0, 0])
    return handoff[None]


def solution(mesh):
    in_specs = (
        P("section", "expert", None),
        P("section", None),
        P("section", "expert", None),
        P("section", "expert", None),
        P("section", "expert", None, None),
        P("section", "expert", None, None),
    )
    out_specs = P("section", "expert", None)
    return jax.shard_map(local, mesh=mesh, in_specs=in_specs, out_specs=out_specs, check_vma=False)
```

time: 410 us -> 143 us (0.35)
  the two profiles are of different devices: /device:TPU:1 before, /device:TPU:72 now
where the time goes in v2:
time: 143 us
  Pallas kernels  141 us (99%)
  local copies, waits for them, and re-layouts  1.82 us (1%)
    pallas_call x1, Pallas kernels, local(): pl.pallas_call(layer_kernel, out_shape=jax.ShapeDtypeStruct((tokens, widt...  141 us

profile of v2, /device:TPU:72, one launch (start us, length us, event | category | flops | bytes accessed | tf_op | source)
XLA Modules:
  0.0 143.1 jit_solution(10569596241599046564)
XLA Ops:
  0.0 141.3 %shard_map.64 = bf16[64,3584]{1,0:T(8,128)(2,1)} custom-call(bf16[64,3584]{1,0:T(8,128)(2,1)} %bitcast.13, f32[1,3584]{1,0:T(1,128)} %gain_hbm.1, s32[2,64]{1,0:T(2,128)} %bitcast.14, f32[2,64]{1,0:T(2,128)} %bitcast.15, bf16[3584,256]{1,0:T(8,128)(2,1)} %bitcast.11, bf16[128,3584]{1,0:T(8,128)(2,1)} %bitcast.12), custom_call_target="tpu_custom_call" | custom-call | flops 2818572288 | bytes 3670016 | tf_op jit(solution)/shard_map/pallas_call | solution.py:414
  141.3 1.8 %copy.8 = bf16[1,64,3584]{2,1,0:T(8,128)(2,1)} copy(bf16[1,64,3584]{2,1,0:T(8,128)(2,1)} %bitcast.10) | data formatting | bytes 917504

commit v3 on v2

--- a/solution.py
+++ b/solution.py
@@ -10,6 +10,8 @@
 PLANES = 4
 SECTIONS = 8
 PIECES = 4
+BACK_PIECES = 7
+AHEAD = 2
 MESH = pl.DeviceIdType.MESH
 BF16 = jnp.bfloat16
 F32 = jnp.float32
@@ -38,6 +40,9 @@
     piece,
     back,
     part,
+    from_below,
+    from_above,
+    total_part,
     home,
     layer_out,
     in_sem,
@@ -55,7 +60,8 @@
     back_send,
     back_recv,
     part_send,
-    part_recv,
+    below_recv,
+    above_recv,
     hand_send,
     hand_recv,
 ):
@@ -64,6 +70,7 @@
     inner = w_down.shape[0]
     slots = EXPERTS * cap
     span = width // PIECES
+    back_span = width // BACK_PIECES
 
     section = lax.axis_index("section")
     me = lax.axis_index("expert")
@@ -91,7 +98,7 @@
         return low + flip * (PLANES - 1 - 2 * low)
 
     def cols(c):
-        return pl.ds(pl.multiple_of(c * span, span), span)
+        return pl.ds(pl.multiple_of(c * back_span, back_span), back_span)
 
     def remote(src, dst, send, recv, to, to_section=None):
         return pltpu.make_async_remote_copy(
@@ -113,7 +120,6 @@
     for d in range(1, EXPERTS):
         greet(in_plane(lax.rem(rank + d, EXPERTS)), section)
     greet(partner, section)
-    greet(me, after)
     greet(me, before)
 
     own_copies = [
@@ -131,7 +137,7 @@
             w_down.at[:, cols(c)], down_w.at[c, pl.ds(0, inner)], in_sem.at[5 + c]
         )
 
-    for c in range(PIECES):
+    for c in range(BACK_PIECES):
         own_down(c).start()
     for copy in own_copies[:4]:
         copy.wait()
@@ -169,7 +175,7 @@
     )
     meta[z, :, tokens : 2 * tokens] = jnp.zeros((8, tokens), F32)
 
-    pl.semaphore_wait(barrier, PLANES - 1 + EXPERTS - 1 + 3)
+    pl.semaphore_wait(barrier, PLANES - 1 + EXPERTS - 1 + 2)
 
     def gate_up_copy(c):
         return remote(
@@ -260,7 +266,7 @@
         return carry
 
     lax.fori_loop(0, PIECES * (PLANES - 1), dispatch, 0)
-    for c in range(PIECES):
+    for c in range(BACK_PIECES):
         down_copy(c).start()
 
     own_copies[4].wait()
@@ -298,11 +304,11 @@
             in_plane(e),
         )
 
-    def down(c, carry):
+    def down(c):
         own_down(c).wait()
         down_copy(c).wait_recv()
         block = jnp.dot(act[...], down_w[c], preferred_element_type=F32).astype(BF16)
-        piece[c] = block.reshape(PLANES, EXPERTS, cap, span)
+        piece[c] = block.reshape(PLANES, EXPERTS, cap, back_span)
 
         def send(i, carry):
             plane = jnp.where(i == PLANES, z, other_plane(PLANES - i))
@@ -312,18 +318,17 @@
             return carry
 
         lax.fori_loop(1, PLANES + 1, send, 0)
-        return carry
-
-    lax.fori_loop(0, PIECES, down, 0)
-
-    def part_copy(c, plane, mine):
-        slot = z if mine else plane
-        return remote(
-            part.at[c, plane],
-            home.at[c, slot],
-            part_send.at[c * PLANES + plane],
-            part_recv.at[c * PLANES + slot],
-            along_z(plane),
+
+    def part_up(c, plane):
+        at = c * PLANES + plane
+        return remote(
+            part.at[c, plane], from_below.at[c, plane], part_send.at[at], below_recv.at[at], me + 1
+        )
+
+    def part_down(c, plane):
+        at = c * PLANES + plane
+        return remote(
+            part.at[c, plane], from_above.at[c, plane], part_send.at[at], above_recv.at[at], me - 1
         )
 
     def combined(c, plane):
@@ -336,11 +341,11 @@
         low = (weight - high.astype(F32)).astype(BF16)
         both = lax.dot_general(
             jnp.concatenate([high, low], axis=1),
-            back[c, plane].reshape(slots, span),
+            back[c, plane].reshape(slots, back_span),
             (((0,), (0,)), ((), ())),
             preferred_element_type=F32,
         )
-        return (both[0:tokens] + both[tokens : 2 * tokens]).astype(BF16)
+        return both[0:tokens] + both[tokens : 2 * tokens]
 
     def hand_copy(c):
         return remote(
@@ -350,52 +355,95 @@
     def combine(c):
         def send(i, carry):
             plane = other_plane(PLANES - i)
-            part[c, plane] = combined(c, plane)
-            part_copy(c, plane, True).start()
+            total_part[...] = combined(c, plane)
+
+            @pl.when((plane > z) & (z > 0))
+            def _():
+                part_up(c, plane).wait_recv()
+                total_part[...] += from_below[c, plane].astype(F32)
+
+            @pl.when((plane < z) & (z < PLANES - 1))
+            def _():
+                part_down(c, plane).wait_recv()
+                total_part[...] += from_above[c, plane].astype(F32)
+
+            part[c, plane] = total_part[...].astype(BF16)
+
+            @pl.when(plane > z)
+            def _():
+                part_up(c, plane).start()
+
+            @pl.when(plane < z)
+            def _():
+                part_down(c, plane).start()
+
             return carry
 
         lax.fori_loop(1, PLANES, send, 0)
-        home[c, z] = combined(c, z)
+        home[c] = hidden[:, cols(c)].astype(F32) + combined(c, z)
 
     def finish(c):
-        for i in range(1, PLANES):
-            part_copy(c, lax.rem(z + i, PLANES), False).wait_recv()
-        total = home[c, 0].astype(F32)
-        for p in range(1, PLANES):
-            total = total + home[c, p].astype(F32)
-        layer_out[c] = (hidden[:, cols(c)].astype(F32) + total).astype(BF16)
+        @pl.when(z > 0)
+        def _():
+            part_up(c, z).wait_recv()
+            home[c] += from_below[c, z].astype(F32)
+
+        @pl.when(z < PLANES - 1)
+        def _():
+            part_down(c, z).wait_recv()
+            home[c] += from_above[c, z].astype(F32)
+
+        layer_out[c] = home[c].astype(BF16)
         hand_copy(c).start()
 
-    def combine_and_finish(c, carry):
+    def way_back(c, carry):
+        @pl.when(c + AHEAD < BACK_PIECES)
+        def _():
+            down(c + AHEAD)
+
         combine(c)
-        finish(c - 1)
+
+        @pl.when(c > 0)
+        def _():
+            finish(c - 1)
+
         return carry
 
-    combine(0)
-    lax.fori_loop(1, PIECES, combine_and_finish, 0)
-    finish(PIECES - 1)
+    for c in range(AHEAD):
+        down(c)
+    lax.fori_loop(0, BACK_PIECES, way_back, 0)
+    finish(BACK_PIECES - 1)
 
     def sent(c, carry):
         gate_up_copy(c).wait_send()
-        down_copy(c).wait_send()
 
         def sent_plane(plane, carry):
             for d in range(1, EXPERTS):
-                e = lax.rem(rank + d, EXPERTS)
-                go_copy(c, plane, e, True).wait_send()
-                back_copy(c, plane, e, True).wait_send()
+                go_copy(c, plane, lax.rem(rank + d, EXPERTS), True).wait_send()
             pass_on(c, plane, lambda copy: copy.wait_send())
             return carry
 
         lax.fori_loop(0, PLANES, sent_plane, 0)
+        return carry
+
+    def sent_back(c, carry):
+        down_copy(c).wait_send()
+
+        def sent_plane(plane, carry):
+            for d in range(1, EXPERTS):
+                back_copy(c, plane, lax.rem(rank + d, EXPERTS), True).wait_send()
+            return carry
+
+        lax.fori_loop(0, PLANES, sent_plane, 0)
         for i in range(1, PLANES):
-            part_copy(c, lax.rem(z + i, PLANES), True).wait_send()
+            part_up(c, lax.rem(z + i, PLANES)).wait_send()
         return carry
 
     lax.fori_loop(0, PIECES, sent, 0)
+    lax.fori_loop(0, BACK_PIECES, sent_back, 0)
     for i in range(1, PLANES):
         meta_copy(lax.rem(z + i, PLANES), z).wait_send()
-    for c in range(PIECES):
+    for c in range(BACK_PIECES):
         hand_copy(c).wait()
 
 
@@ -406,11 +454,14 @@
     cap = tokens * picks // EXPERTS
     inner = w_down.shape[2]
     span = width // PIECES
+    back_span = width // BACK_PIECES
     slots = EXPERTS * cap
     hbm = pl.BlockSpec(memory_space=pltpu.HBM)
     dma = pltpu.SemaphoreType.DMA
     blocks = pltpu.VMEM((PIECES, PLANES, EXPERTS, cap, span), BF16)
     per_plane = pltpu.VMEM((PIECES, PLANES, tokens, span), BF16)
+    back_blocks = pltpu.VMEM((BACK_PIECES, PLANES, EXPERTS, cap, back_span), BF16)
+    back_per_plane = pltpu.VMEM((BACK_PIECES, PLANES, tokens, back_span), BF16)
     handoff = pl.pallas_call(
         layer_kernel,
         out_shape=jax.ShapeDtypeStruct((tokens, width), BF16),
@@ -426,19 +477,22 @@
             blocks,
             blocks,
             pltpu.VMEM((2, width, 2 * inner), BF16),
-            pltpu.VMEM((PIECES, 2 * inner, span), BF16),
+            pltpu.VMEM((BACK_PIECES, 2 * inner, back_span), BF16),
             pltpu.VMEM((2, PLANES * slots, 2 * inner), F32),
             pltpu.VMEM((PLANES * slots, 2 * inner), BF16),
-            blocks,
-            blocks,
-            per_plane,
-            per_plane,
-            pltpu.VMEM((PIECES, tokens, span), BF16),
-            dma((5 + PIECES,)),
+            back_blocks,
+            back_blocks,
+            back_per_plane,
+            back_per_plane,
+            back_per_plane,
+            pltpu.VMEM((tokens, back_span), F32),
+            pltpu.VMEM((BACK_PIECES, tokens, back_span), F32),
+            pltpu.VMEM((BACK_PIECES, tokens, back_span), BF16),
+            dma((5 + BACK_PIECES,)),
             dma((PIECES,)),
             dma((PIECES,)),
-            dma((PIECES,)),
-            dma((PIECES,)),
+            dma((BACK_PIECES,)),
+            dma((BACK_PIECES,)),
             dma((PIECES * PLANES,)),
             dma((PIECES * PLANES,)),
             dma((PIECES * PLANES,)),
@@ -446,12 +500,13 @@
             dma((PLANES,)),
             dma((PIECES * PLANES * EXPERTS,)),
             dma((PIECES * PLANES * EXPERTS,)),
-            dma((PIECES * PLANES * EXPERTS,)),
-            dma((PIECES * PLANES * EXPERTS,)),
-            dma((PIECES * PLANES,)),
-            dma((PIECES * PLANES,)),
-            dma((PIECES,)),
-            dma((PIECES,)),
+            dma((BACK_PIECES * PLANES * EXPERTS,)),
+            dma((BACK_PIECES * PLANES * EXPERTS,)),
+            dma((BACK_PIECES * PLANES,)),
+            dma((BACK_PIECES * PLANES,)),
+            dma((BACK_PIECES * PLANES,)),
+            dma((BACK_PIECES,)),
+            dma((BACK_PIECES,)),
         ],
         compiler_params=pltpu.CompilerParams(
             collective_id=0, has_side_effects=True, vmem_limit_bytes=62 * 1024 * 1024

time: 143 us -> 126 us (0.88)
  the two profiles are of different devices: /device:TPU:72 before, /device:TPU:64 now
where the time goes in v3:
time: 126 us
  Pallas kernels  124 us (98%)
  local copies, waits for them, and re-layouts  1.82 us (1%)
    pallas_call x1, Pallas kernels, local(): pl.pallas_call(layer_kernel, out_shape=jax.ShapeDtypeStruct((tokens, widt...  124 us

profile of v3, /device:TPU:64, one launch (start us, length us, event | category | flops | bytes accessed | tf_op | source)
XLA Modules:
  0.0 126.0 jit_solution(7360201325816878893)
XLA Ops:
  0.0 124.2 %shard_map.64 = bf16[64,3584]{1,0:T(8,128)(2,1)} custom-call(bf16[64,3584]{1,0:T(8,128)(2,1)} %bitcast.13, f32[1,3584]{1,0:T(1,128)} %gain_hbm.1, s32[2,64]{1,0:T(2,128)} %bitcast.14, f32[2,64]{1,0:T(2,128)} %bitcast.15, bf16[3584,256]{1,0:T(8,128)(2,1)} %bitcast.11, bf16[128,3584]{1,0:T(8,128)(2,1)} %bitcast.12), custom_call_target="tpu_custom_call" | custom-call | flops 2818572288 | bytes 3670016 | tf_op jit(solution)/shard_map/pallas_call | solution.py:465
  124.2 1.8 %copy.8 = bf16[1,64,3584]{2,1,0:T(8,128)(2,1)} copy(bf16[1,64,3584]{2,1,0:T(8,128)(2,1)} %bitcast.10) | data formatting | bytes 917504

commit v4 on v3

--- a/solution.py
+++ b/solution.py
@@ -12,6 +12,7 @@
 PIECES = 4
 BACK_PIECES = 7
 AHEAD = 2
+DOWN_AHEAD = 3
 MESH = pl.DeviceIdType.MESH
 BF16 = jnp.bfloat16
 F32 = jnp.float32
@@ -110,6 +111,9 @@
             device_id_type=MESH,
         )
 
+    others = [lax.rem(rank + d, EXPERTS) for d in range(1, EXPERTS)]
+    plane_peers = [(e, in_plane(e)) for e in others]
+
     barrier = pltpu.get_barrier_semaphore()
 
     def greet(to, to_section):
@@ -117,8 +121,8 @@
 
     for i in range(1, PLANES):
         greet(along_z(lax.rem(z + i, PLANES)), section)
-    for d in range(1, EXPERTS):
-        greet(in_plane(lax.rem(rank + d, EXPERTS)), section)
+    for _, to in plane_peers:
+        greet(to, section)
     greet(partner, section)
     greet(me, before)
 
@@ -217,15 +221,25 @@
         def _():
             act_on(dn_copy(c, plane))
 
-    def go_copy(c, plane, e, mine):
-        slot = rank if mine else e
-        at = (c * PLANES + plane) * EXPERTS
+    def go_copy(c, plane, e, to):
+        at = c * PLANES + plane
         return remote(
             sorted_rows.at[c, plane, e],
-            rows.at[c, plane, slot],
-            go_send.at[at + e],
-            go_recv.at[at + slot],
-            in_plane(e),
+            rows.at[c, plane, rank],
+            go_send.at[at],
+            go_recv.at[at],
+            to,
+        )
+
+    def go_all(c, plane):
+        at = c * PLANES + plane
+        blocks = pl.ds(0, EXPERTS - 1)
+        return remote(
+            sorted_rows.at[c, plane, blocks],
+            rows.at[c, plane, blocks],
+            go_send.at[at],
+            go_recv.at[at],
+            me,
         )
 
     slot_row = lax.broadcasted_iota(jnp.int32, (slots, tokens), 0).astype(F32)
@@ -237,8 +251,8 @@
         ).astype(BF16)
         block = jnp.dot(placed, raw[c, plane], preferred_element_type=F32).astype(BF16)
         sorted_rows[c, plane] = block.reshape(EXPERTS, cap, span)
-        for d in range(1, EXPERTS):
-            go_copy(c, plane, lax.rem(rank + d, EXPERTS), True).start()
+        for e, to in plane_peers:
+            go_copy(c, plane, e, to).start()
         rows[c, plane, rank] = sorted_rows[c, plane, rank]
 
     for i in range(1, PLANES):
@@ -266,15 +280,16 @@
         return carry
 
     lax.fori_loop(0, PIECES * (PLANES - 1), dispatch, 0)
-    for c in range(BACK_PIECES):
+    for c in range(PIECES):
+        gate_up_copy(c).wait_send()
+    for c in range(DOWN_AHEAD):
         down_copy(c).start()
 
     own_copies[4].wait()
 
     def gate_up(c, carry):
         def arrived(plane, carry):
-            for d in range(1, EXPERTS):
-                go_copy(c, plane, lax.rem(rank + d, EXPERTS), False).wait_recv()
+            go_all(c, plane).wait_recv()
             return carry
 
         lax.fori_loop(0, PLANES, arrived, 0)
@@ -293,27 +308,42 @@
             gate / (1.0 + jnp.exp(-gate)) * total_gate_up[s, :, inner : 2 * inner]
         ).astype(BF16)
 
-    def back_copy(c, plane, e, mine):
-        slot = rank if mine else e
-        at = (c * PLANES + plane) * EXPERTS
+    def back_copy(c, plane, e, to):
+        at = c * PLANES + plane
         return remote(
             piece.at[c, plane, e],
-            back.at[c, plane, slot],
-            back_send.at[at + e],
-            back_recv.at[at + slot],
-            in_plane(e),
+            back.at[c, plane, rank],
+            back_send.at[at],
+            back_recv.at[at],
+            to,
+        )
+
+    def back_all(c, plane):
+        at = c * PLANES + plane
+        blocks = pl.ds(0, EXPERTS - 1)
+        return remote(
+            piece.at[c, plane, blocks],
+            back.at[c, plane, blocks],
+            back_send.at[at],
+            back_recv.at[at],
+            me,
         )
 
     def down(c):
         own_down(c).wait()
         down_copy(c).wait_recv()
+
+        @pl.when(c + DOWN_AHEAD < BACK_PIECES)
+        def _():
+            down_copy(c + DOWN_AHEAD).start()
+
         block = jnp.dot(act[...], down_w[c], preferred_element_type=F32).astype(BF16)
         piece[c] = block.reshape(PLANES, EXPERTS, cap, back_span)
 
         def send(i, carry):
             plane = jnp.where(i == PLANES, z, other_plane(PLANES - i))
-            for d in range(1, EXPERTS):
-                back_copy(c, plane, lax.rem(rank + d, EXPERTS), True).start()
+            for e, to in plane_peers:
+                back_copy(c, plane, e, to).start()
             back[c, plane, rank] = piece[c, plane, rank]
             return carry
 
@@ -332,8 +362,7 @@
         )
 
     def combined(c, plane):
-        for d in range(1, EXPERTS):
-            back_copy(c, plane, lax.rem(rank + d, EXPERTS), False).wait_recv()
+        back_all(c, plane).wait_recv()
         weight = jnp.where(
             slot_row == meta[plane, 0:1, 0:tokens], meta[plane, 2:3, 0:tokens], 0.0
         ) + jnp.where(slot_row == meta[plane, 1:2, 0:tokens], meta[plane, 3:4, 0:tokens], 0.0)
@@ -396,53 +425,49 @@
         layer_out[c] = home[c].astype(BF16)
         hand_copy(c).start()
 
-    def way_back(c, carry):
-        @pl.when(c + AHEAD < BACK_PIECES)
-        def _():
-            down(c + AHEAD)
-
-        combine(c)
-
-        @pl.when(c > 0)
-        def _():
-            finish(c - 1)
-
-        return carry
-
-    for c in range(AHEAD):
-        down(c)
-    lax.fori_loop(0, BACK_PIECES, way_back, 0)
-    finish(BACK_PIECES - 1)
-
-    def sent(c, carry):
-        gate_up_copy(c).wait_send()
-
+    def dispatch_left(c, carry):
         def sent_plane(plane, carry):
-            for d in range(1, EXPERTS):
-                go_copy(c, plane, lax.rem(rank + d, EXPERTS), True).wait_send()
+            go_all(c, plane).wait_send()
             pass_on(c, plane, lambda copy: copy.wait_send())
             return carry
 
         lax.fori_loop(0, PLANES, sent_plane, 0)
         return carry
 
-    def sent_back(c, carry):
+    def back_left(c):
         down_copy(c).wait_send()
 
         def sent_plane(plane, carry):
-            for d in range(1, EXPERTS):
-                back_copy(c, plane, lax.rem(rank + d, EXPERTS), True).wait_send()
+            back_all(c, plane).wait_send()
             return carry
 
         lax.fori_loop(0, PLANES, sent_plane, 0)
         for i in range(1, PLANES):
             part_up(c, lax.rem(z + i, PLANES)).wait_send()
+
+    def way_back(c, carry):
+        @pl.when(c + AHEAD < BACK_PIECES)
+        def _():
+            down(c + AHEAD)
+
+        combine(c)
+
+        @pl.when(c > 0)
+        def _():
+            finish(c - 1)
+            back_left(c - 1)
+
         return carry
 
-    lax.fori_loop(0, PIECES, sent, 0)
-    lax.fori_loop(0, BACK_PIECES, sent_back, 0)
+    for c in range(AHEAD):
+        down(c)
+    lax.fori_loop(0, PIECES, dispatch_left, 0)
     for i in range(1, PLANES):
         meta_copy(lax.rem(z + i, PLANES), z).wait_send()
+    lax.fori_loop(0, BACK_PIECES, way_back, 0)
+    finish(BACK_PIECES - 1)
+    back_left(BACK_PIECES - 1)
+
     for c in range(BACK_PIECES):
         hand_copy(c).wait()
 
@@ -498,10 +523,10 @@
             dma((PIECES * PLANES,)),
             dma((PLANES,)),
             dma((PLANES,)),
-            dma((PIECES * PLANES * EXPERTS,)),
-            dma((PIECES * PLANES * EXPERTS,)),
-            dma((BACK_PIECES * PLANES * EXPERTS,)),
-            dma((BACK_PIECES * PLANES * EXPERTS,)),
+            dma((PIECES * PLANES,)),
+            dma((PIECES * PLANES,)),
+            dma((BACK_PIECES * PLANES,)),
+            dma((BACK_PIECES * PLANES,)),
             dma((BACK_PIECES * PLANES,)),
             dma((BACK_PIECES * PLANES,)),
             dma((BACK_PIECES * PLANES,)),

time: 126 us -> 121 us (0.960)
  the two profiles are of different devices: /device:TPU:64 before, /device:TPU:352 now
where the time goes in v4:
time: 121 us
  Pallas kernels  119 us (98%)
  local copies, waits for them, and re-layouts  1.82 us (2%)
    pallas_call x1, Pallas kernels, local(): pl.pallas_call(layer_kernel, out_shape=jax.ShapeDtypeStruct((tokens, widt...  119 us

profile of v4, /device:TPU:352, one launch (start us, length us, event | category | flops | bytes accessed | tf_op | source)
XLA Modules:
  0.0 120.9 jit_solution(1067338206120098892)
XLA Ops:
  0.0 119.1 %shard_map.64 = bf16[64,3584]{1,0:T(8,128)(2,1)} custom-call(bf16[64,3584]{1,0:T(8,128)(2,1)} %bitcast.13, f32[1,3584]{1,0:T(1,128)} %gain_hbm.1, s32[2,64]{1,0:T(2,128)} %bitcast.14, f32[2,64]{1,0:T(2,128)} %bitcast.15, bf16[3584,256]{1,0:T(8,128)(2,1)} %bitcast.11, bf16[128,3584]{1,0:T(8,128)(2,1)} %bitcast.12), custom_call_target="tpu_custom_call" | custom-call | flops 2818572288 | bytes 3670016 | tf_op jit(solution)/shard_map/pallas_call | solution.py:490
  119.1 1.8 %copy.8 = bf16[1,64,3584]{2,1,0:T(8,128)(2,1)} copy(bf16[1,64,3584]{2,1,0:T(8,128)(2,1)} %bitcast.10) | data formatting | bytes 917504

commit v5 on v4

--- a/solution.py
+++ b/solution.py
@@ -13,6 +13,7 @@
 BACK_PIECES = 7
 AHEAD = 2
 DOWN_AHEAD = 3
+HOP_STEPS = 1
 MESH = pl.DeviceIdType.MESH
 BF16 = jnp.bfloat16
 F32 = jnp.float32
@@ -382,34 +383,56 @@
         )
 
     def combine(c):
-        def send(i, carry):
+        def one(i, carry):
             plane = other_plane(PLANES - i)
-            total_part[...] = combined(c, plane)
-
-            @pl.when((plane > z) & (z > 0))
+            total_part[c, plane] = combined(c, plane)
+
+            @pl.when((plane > z) & (z == 0))
+            def _():
+                part[c, plane] = total_part[c, plane].astype(BF16)
+                part_up(c, plane).start()
+
+            @pl.when((plane < z) & (z == PLANES - 1))
+            def _():
+                part[c, plane] = total_part[c, plane].astype(BF16)
+                part_down(c, plane).start()
+
+            return carry
+
+        lax.fori_loop(1, PLANES, one, 0)
+        home[c] = hidden[:, cols(c)].astype(F32) + combined(c, z)
+
+    def add_up(c):
+        def one(i, carry):
+            plane = other_plane(PLANES - i)
+
+            @pl.when(plane > z)
             def _():
                 part_up(c, plane).wait_recv()
-                total_part[...] += from_below[c, plane].astype(F32)
-
-            @pl.when((plane < z) & (z < PLANES - 1))
+                part[c, plane] = (
+                    total_part[c, plane] + from_below[c, plane].astype(F32)
+                ).astype(BF16)
+                part_up(c, plane).start()
+
+            return carry
+
+        lax.fori_loop(1, PLANES, one, 0)
+
+    def add_down(c):
+        def one(i, carry):
+            plane = other_plane(PLANES - i)
+
+            @pl.when(plane < z)
             def _():
                 part_down(c, plane).wait_recv()
-                total_part[...] += from_above[c, plane].astype(F32)
-
-            part[c, plane] = total_part[...].astype(BF16)
-
-            @pl.when(plane > z)
-            def _():
-                part_up(c, plane).start()
-
-            @pl.when(plane < z)
-            def _():
+                part[c, plane] = (
+                    total_part[c, plane] + from_above[c, plane].astype(F32)
+                ).astype(BF16)
                 part_down(c, plane).start()
 
             return carry
 
-        lax.fori_loop(1, PLANES, send, 0)
-        home[c] = hidden[:, cols(c)].astype(F32) + combined(c, z)
+        lax.fori_loop(1, PLANES, one, 0)
 
     def finish(c):
         @pl.when(z > 0)
@@ -445,17 +468,33 @@
         for i in range(1, PLANES):
             part_up(c, lax.rem(z + i, PLANES)).wait_send()
 
-    def way_back(c, carry):
-        @pl.when(c + AHEAD < BACK_PIECES)
-        def _():
-            down(c + AHEAD)
-
-        combine(c)
-
-        @pl.when(c > 0)
-        def _():
-            finish(c - 1)
-            back_left(c - 1)
+    hops_up, hops_down = z * HOP_STEPS, (PLANES - 1 - z) * HOP_STEPS
+    hops_home = (PLANES - 1 - z_low) * HOP_STEPS
+
+    def way_back(n, carry):
+        @pl.when(n + AHEAD < BACK_PIECES)
+        def _():
+            down(n + AHEAD)
+
+        @pl.when(n < BACK_PIECES)
+        def _():
+            combine(n)
+
+        @pl.when((z > 0) & (z < PLANES - 1) & (n >= hops_up) & (n - hops_up < BACK_PIECES))
+        def _():
+            add_up(n - hops_up)
+
+        @pl.when((z > 0) & (z < PLANES - 1) & (n >= hops_down) & (n - hops_down < BACK_PIECES))
+        def _():
+            add_down(n - hops_down)
+
+        @pl.when((n >= hops_home) & (n - hops_home < BACK_PIECES))
+        def _():
+            finish(n - hops_home)
+
+        @pl.when((n > hops_home) & (n - hops_home <= BACK_PIECES))
+        def _():
+            back_left(n - hops_home - 1)
 
         return carry
 
@@ -464,9 +503,7 @@
     lax.fori_loop(0, PIECES, dispatch_left, 0)
     for i in range(1, PLANES):
         meta_copy(lax.rem(z + i, PLANES), z).wait_send()
-    lax.fori_loop(0, BACK_PIECES, way_back, 0)
-    finish(BACK_PIECES - 1)
-    back_left(BACK_PIECES - 1)
+    lax.fori_loop(0, BACK_PIECES + (PLANES - 1) * HOP_STEPS + 1, way_back, 0)
 
     for c in range(BACK_PIECES):
         hand_copy(c).wait()
@@ -510,7 +547,7 @@
             back_per_plane,
             back_per_plane,
             back_per_plane,
-            pltpu.VMEM((tokens, back_span), F32),
+            pltpu.VMEM((BACK_PIECES, PLANES, tokens, back_span), F32),
             pltpu.VMEM((BACK_PIECES, tokens, back_span), F32),
             pltpu.VMEM((BACK_PIECES, tokens, back_span), BF16),
             dma((5 + BACK_PIECES,)),

time: 121 us -> 122 us (level)
  the two profiles are of different devices: /device:TPU:352 before, /device:TPU:1 now
where the time goes in v5:
time: 122 us; the launch traced here: 120 us
  Pallas kernels  119 us (98%)
  local copies, waits for them, and re-layouts  1.82 us (1%)
    pallas_call x1, Pallas kernels, local(): pl.pallas_call(layer_kernel, out_shape=jax.ShapeDtypeStruct((tokens, widt...  119 us

profile of v5, /device:TPU:1, one launch (start us, length us, event | category | flops | bytes accessed | tf_op | source)
XLA Modules:
  0.0 120.5 jit_solution(2301526638698728747)
XLA Ops:
  0.0 118.7 %shard_map.64 = bf16[64,3584]{1,0:T(8,128)(2,1)} custom-call(bf16[64,3584]{1,0:T(8,128)(2,1)} %bitcast.13, f32[1,3584]{1,0:T(1,128)} %gain_hbm.1, s32[2,64]{1,0:T(2,128)} %bitcast.14, f32[2,64]{1,0:T(2,128)} %bitcast.15, bf16[3584,256]{1,0:T(8,128)(2,1)} %bitcast.11, bf16[128,3584]{1,0:T(8,128)(2,1)} %bitcast.12), custom_call_target="tpu_custom_call" | custom-call | flops 2818572288 | bytes 3670016 | tf_op jit(solution)/shard_map/pallas_call | solution.py:527
  118.7 1.8 %copy.8 = bf16[1,64,3584]{2,1,0:T(8,128)(2,1)} copy(bf16[1,64,3584]{2,1,0:T(8,128)(2,1)} %bitcast.10) | data formatting | bytes 917504

commit v6 on v4

--- a/solution.py
+++ b/solution.py
@@ -46,6 +46,7 @@
     total_part,
     home,
     layer_out,
+    gate_matrix,
     in_sem,
     gu_send,
     gu_recv,
@@ -285,6 +286,17 @@
     for c in range(DOWN_AHEAD):
         down_copy(c).start()
 
+    def gate_rows(plane, carry):
+        weight = jnp.where(
+            slot_row == meta[plane, 0:1, 0:tokens], meta[plane, 2:3, 0:tokens], 0.0
+        ) + jnp.where(slot_row == meta[plane, 1:2, 0:tokens], meta[plane, 3:4, 0:tokens], 0.0)
+        high = weight.astype(BF16)
+        low = (weight - high.astype(F32)).astype(BF16)
+        both = jnp.concatenate([high.astype(F32), low.astype(F32)], axis=1)
+        gate_matrix[plane] = jnp.transpose(both).astype(BF16)
+        return carry
+
+    lax.fori_loop(0, PLANES, gate_rows, 0)
     own_copies[4].wait()
 
     def gate_up(c, carry):
@@ -363,15 +375,9 @@
 
     def combined(c, plane):
         back_all(c, plane).wait_recv()
-        weight = jnp.where(
-            slot_row == meta[plane, 0:1, 0:tokens], meta[plane, 2:3, 0:tokens], 0.0
-        ) + jnp.where(slot_row == meta[plane, 1:2, 0:tokens], meta[plane, 3:4, 0:tokens], 0.0)
-        high = weight.astype(BF16)
-        low = (weight - high.astype(F32)).astype(BF16)
-        both = lax.dot_general(
-            jnp.concatenate([high, low], axis=1),
+        both = jnp.dot(
+            gate_matrix[plane],
             back[c, plane].reshape(slots, back_span),
-            (((0,), (0,)), ((), ())),
             preferred_element_type=F32,
         )
         return both[0:tokens] + both[tokens : 2 * tokens]
@@ -513,6 +519,7 @@
             pltpu.VMEM((tokens, back_span), F32),
             pltpu.VMEM((BACK_PIECES, tokens, back_span), F32),
             pltpu.VMEM((BACK_PIECES, tokens, back_span), BF16),
+            pltpu.VMEM((PLANES, 2 * tokens, slots), BF16),
             dma((5 + BACK_PIECES,)),
             dma((PIECES,)),
             dma((PIECES,)),

time: 121 us -> 121 us (level)
  the two profiles are of different devices: /device:TPU:352 before, /device:TPU:1 now
where the time goes in v6:
time: 121 us; the launch traced here: 120 us
  Pallas kernels  119 us (98%)
  local copies, waits for them, and re-layouts  1.82 us (2%)
    pallas_call x1, Pallas kernels, local(): pl.pallas_call(layer_kernel, out_shape=jax.ShapeDtypeStruct((tokens, widt...  119 us

profile of v6, /device:TPU:1, one launch (start us, length us, event | category | flops | bytes accessed | tf_op | source)
XLA Modules:
  0.0 120.5 jit_solution(13945899379777013251)
XLA Ops:
  0.0 118.6 %shard_map.64 = bf16[64,3584]{1,0:T(8,128)(2,1)} custom-call(bf16[64,3584]{1,0:T(8,128)(2,1)} %bitcast.13, f32[1,3584]{1,0:T(1,128)} %gain_hbm.1, s32[2,64]{1,0:T(2,128)} %bitcast.14, f32[2,64]{1,0:T(2,128)} %bitcast.15, bf16[3584,256]{1,0:T(8,128)(2,1)} %bitcast.11, bf16[128,3584]{1,0:T(8,128)(2,1)} %bitcast.12), custom_call_target="tpu_custom_call" | custom-call | flops 2818572288 | bytes 3670016 | tf_op jit(solution)/shard_map/pallas_call | solution.py:496
  118.7 1.8 %copy.8 = bf16[1,64,3584]{2,1,0:T(8,128)(2,1)} copy(bf16[1,64,3584]{2,1,0:T(8,128)(2,1)} %bitcast.10) | data formatting | bytes 917504
